TPU v7x, 256 devices: a whole 4x4x8 slice. The times are simulated.
256 devices in a mesh: grp: 32 (over z_lo, x, core), tp: 8 (over y, z_hi).
Axes of the slice: x: 4, y: 4, z: 8 (z_hi: 2, z_lo: 4; z = z_hi * 4 + z_lo), core: 2. Of those that a mesh axis runs over, the one named last changes fastest.
Arguments:
- states: bfloat16 [2, 2048, 8192], P(None, 'grp', 'tp'), may hold values from -6 to 6
- cache: bfloat16 [2, 2048, 8, 128, 128], P(None, 'grp', 'tp'), may hold values from -256 to 256
- lengths: int32 [2048], P('grp'), may hold values from 32 to 128, as said below
- plan: int32 [32], replicated, may hold values from 0 to 31, each once
- wq_new: bfloat16 [8192, 4096], P('grp', 'tp'), may hold values from -0.0625 to 0.0625
- wkv_new: bfloat16 [2, 8192, 1024], P(None, 'grp', 'tp'), may hold values from -0.0625 to 0.0625
- wo_new: bfloat16 [4096, 8192], P('tp', 'grp'), may hold values from -0.09375 to 0.09375
Outputs:
- attended: bfloat16 [2, 2048, 8192], P(None, 'grp', 'tp')
- new_kv: bfloat16 [2, 2, 2048, 8, 128], P(None, None, 'grp', 'tp')
Inputs may be any that keep to these rules, and one draw needn't show every extreme that they name: `plan`: a permutation of the owners. `lengths`: some row of every draw has exactly 128.
All inputs are finite; a program needn't handle non-finite values.
Results may differ from a plain program's by a relative error of at most 0.017.
Values may be sent and summed in bfloat16 or wider, within the bound.
A program may use at most 128 MiB of HBM per device.

v0:
```python
import jax
import jax.numpy as jnp
from jax import lax
from jax.sharding import PartitionSpec as P


def on_device(states, cache, lengths, plan, wq_new, wkv_new, wo_new):
    gathered = lax.all_gather(states, "tp", axis=2, tiled=True)
    steps_count, rows, width = gathered.shape
    widened = gathered.astype(jnp.float32)
    normed = (
        widened * lax.rsqrt(jnp.mean(widened * widened, axis=-1, keepdims=True) + 1e-05)
    ).astype(jnp.bfloat16)
    flattened = normed.reshape(steps_count * rows, width)
    owners = plan.shape[0]
    block_width = width // owners
    permuted = jnp.take(flattened.reshape(steps_count * rows, owners, block_width), plan, axis=1)
    permuted = permuted.reshape(steps_count * rows, width)
    query_cols = wq_new.shape[1]
    kv_cols = wkv_new.shape[2]
    head_size = cache.shape[-1]
    kv_heads = kv_cols // head_size
    group = query_cols // head_size // kv_heads

    def matching():
        return permuted

    query_sum = jnp.dot(
        matching(),
        lax.all_gather(wq_new, "grp", axis=0, tiled=True),
        preferred_element_type=jnp.float32,
    )
    left = matching()
    key_sum = jnp.dot(
        left,
        lax.all_gather(wkv_new[0], "grp", axis=0, tiled=True),
        preferred_element_type=jnp.float32,
    )
    value_sum = jnp.dot(
        left,
        lax.all_gather(wkv_new[1], "grp", axis=0, tiled=True),
        preferred_element_type=jnp.float32,
    )
    query = query_sum.astype(jnp.bfloat16).reshape(steps_count, rows, kv_heads, group, head_size)
    key_new = key_sum.astype(jnp.bfloat16).reshape(steps_count, rows, kv_heads, head_size)
    value_new = value_sum.astype(jnp.bfloat16).reshape(steps_count, rows, kv_heads, head_size)
    new_kv = jnp.stack([key_new, value_new], axis=1)
    scale = 1.0 / head_size**0.5
    slots_count = cache.shape[3]
    scores = (
        jnp.einsum("srkgd,rkpd->srkgp", query, cache[0], preferred_element_type=jnp.float32) * scale
    )
    slots = lax.broadcasted_iota(jnp.int32, (rows, slots_count), 1)
    valid = (slots < lengths[:, None])[None, :, None, None, :]
    scores = jnp.where(valid, scores, -1e30)
    own = (
        jnp.einsum("srkgd,trkd->srkgt", query, key_new, preferred_element_type=jnp.float32) * scale
    )
    step_ids = lax.broadcasted_iota(jnp.int32, (2, 1, 1, 1, 2), 0)
    key_ids = lax.broadcasted_iota(jnp.int32, (2, 1, 1, 1, 2), 4)
    own = jnp.where(key_ids <= step_ids, own, -1e30)
    top = jnp.maximum(jnp.max(scores, axis=-1, keepdims=True), jnp.max(own, axis=-1, keepdims=True))
    cached_exp = jnp.exp(scores - top)
    own_exp = jnp.exp(own - top)
    total = jnp.sum(cached_exp, axis=-1, keepdims=True) + jnp.sum(own_exp, axis=-1, keepdims=True)
    cached_weight = (cached_exp / total).astype(jnp.bfloat16)
    own_weight = (own_exp / total).astype(jnp.bfloat16)
    heads = jnp.einsum(
        "srkgp,rkpd->srkgd", cached_weight, cache[1], preferred_element_type=jnp.float32
    )
    heads = heads + jnp.einsum(
        "srkgt,trkd->srkgd", own_weight, value_new, preferred_element_type=jnp.float32
    )
    heads = heads.astype(jnp.bfloat16).reshape(steps_count * rows, query_cols)
    stored_order = jnp.dot(
        heads, lax.all_gather(wo_new, "grp", axis=1, tiled=True), preferred_element_type=jnp.float32
    )
    inverse = jnp.argsort(plan)
    true_order = jnp.take(
        stored_order.reshape(steps_count * rows, owners, block_width), inverse, axis=1
    )
    true_order = true_order.reshape(steps_count, rows, width)
    attended = lax.psum_scatter(
        true_order.astype(jnp.bfloat16), "tp", scatter_dimension=2, tiled=True
    )
    return (attended, new_kv)


def solution(mesh):
    return jax.shard_map(
        on_device,
        mesh=mesh,
        in_specs=(
            P(None, "grp", "tp"),
            P(None, "grp", "tp", None, None),
            P("grp"),
            P(),
            P("grp", "tp"),
            P(None, "grp", "tp"),
            P("tp", "grp"),
        ),
        out_specs=(P(None, "grp", "tp"), P(None, None, "grp", "tp", None)),
        check_vma=False,
    )
```

profile of v0, /device:TPU:1, one launch (start us, length us, event | category | flops | bytes accessed | tf_op | source)
XLA Modules:
  0.0 497.4 jit_solution(13743421720127614732)
XLA Ops:
  7.2 0.7 all-gather.8.cloned.1.call-update
  7.9 1.5 fusion.35
  9.5 0.7 all-gather.16.cloned.1.call-update
  11.4 0.7 compare_and_fusion
  12.2 2.3 sort.17
  14.6 0.7 compare_select_fusion
  15.3 0.7 iota_compare_fusion
  16.0 73.3 %all-gather.8.cloned.1.call-done = bf16[2,64,8192]{2,1,0:T(8,128)(2,1)} async-done(((bf16[2,64,1024]{2,1,0:T(8,128)(2,1)}), bf16[2,64,8192]{2,1,0:T(8,128)(2,1)}) %all-gather.8.cloned.1.call-update) | async-done | bytes 2097168 | tf_op jit(solution)/shard_map/all_gather | solution.py:8
  89.4 2.3 fusion
  92.1 0.6 copy.50
  92.7 1.2 copy.29
  93.9 2.0 gather_fusion
  95.9 4.1 copy.30
  99.9 5.8 %bitcast_select_fusion = bf16[128,8192]{0,1:T(8,128)(2,1)S(1)} fusion(bf16[128,32,256]{0,2,1:T(8,128)(2,1)} %copy.30, pred[8192]{0:T(1024)(128)(4,1)S(1)} %broadcast_in_dim.68), kind=kLoop, calls=%fused_computation.15 | loop fusion | flops 1048576 | bytes 4202496 | tf_op jit(solution)/shard_map/jit(_take)/select_n | solution.py:17
  105.8 43.4 %all-gather.14.cloned.1.call-done = bf16[1,8192,128]{2,1,0:T(8,128)(2,1)} async-done(((bf16[1,256,128]{2,1,0:T(8,128)(2,1)}), bf16[1,8192,128]{2,1,0:T(8,128)(2,1)}) %all-gather.14.cloned.1.call-update) | async-done | bytes 2097168 | tf_op jit(solution)/shard_map/all_gather | solution.py:36
  149.2 2.3 fusion.15
  151.6 59.2 %all-gather.16.cloned.1.call-done = bf16[1,8192,128]{2,1,0:T(8,128)(2,1)} async-done(((bf16[1,256,128]{2,1,0:T(8,128)(2,1)}), bf16[1,8192,128]{2,1,0:T(8,128)(2,1)}) %all-gather.16.cloned.1.call-update) | async-done | bytes 2097168 | tf_op jit(solution)/shard_map/all_gather | solution.py:41
  210.8 2.3 fusion.18
  213.1 67.4 %all-gather.10.cloned.1.call-done = bf16[8192,512]{1,0:T(8,128)(2,1)} async-done(((bf16[256,512]{1,0:T(8,128)(2,1)}), bf16[8192,512]{1,0:T(8,128)(2,1)}) %all-gather.10.cloned.1.call-update) | async-done | bytes 8388624 | tf_op jit(solution)/shard_map/all_gather | solution.py:30
  280.5 4.7 convolution_convert_fusion
  285.3 1.3 fusion.37
  286.6 3.1 fusion.36
  290.8 0.7 fusion.13
  291.6 76.7 %all-gather.12.cloned.1.call-done = bf16[512,8192]{1,0:T(8,128)(2,1)} async-done(((bf16[512,256]{1,0:T(8,128)(2,1)}), bf16[512,8192]{1,0:T(8,128)(2,1)}) %all-gather.12.cloned.1.call-update) | async-done | bytes 8388624 | tf_op jit(solution)/shard_map/all_gather | solution.py:76
  368.3 11.9 %copy.38 = bf16[8192,512]{1,0:T(8,128)(2,1)} copy(bf16[8192,512]{0,1:T(8,128)(2,1)} %bitcast.109) | data formatting | bytes 16777216 | tf_op jit(solution)/shard_map/dot_general | solution.py:75
  380.2 7.5 %fusion.38 = bf16[128,32,256]{2,0,1:T(8,128)(2,1)} fusion(bf16[128,512,1]{1,0,2:T(8,128)(2,1)S(1)} %reshape.167, bf16[32,256,512]{2,1,0:T(8,128)(2,1)} %bitcast.107), kind=kOutput, calls=%fused_computation.58 | convolution fusion | flops 1073741824 | bytes 10616832 | tf_op jit(solution)/shard_map/dot_general | solution.py:75
  387.8 2.3 gather_fusion.1
  390.1 2.5 copy.39
  392.6 2.9 gather.15
  395.5 1.8 select_convert_fusion
  397.3 0.6 pad_maximum_fusion
  397.9 92.6 %reduce-scatter.2.cloned.1.call-done = bf16[2,64,1024]{2,1,0:T(8,128)(2,1)} async-done(((bf16[2,64,8192]{2,1,0:T(8,128)(2,1)}), bf16[2,64,1024]{2,1,0:T(8,128)(2,1)}) %reduce-scatter.2.cloned.1.call-update) | async-done | bytes 262160 | tf_op jit(solution)/shard_map/reduce_scatter | solution.py:83
  (34 shorter events, 3.3 us)
Async XLA Ops:
  7.2 82.2 %all-gather.8.cloned.1.call-start = ((), (), s32[]{:S(2)}) async-start(), calls=%async_computation.1 | async-start | bytes 2359296 | tf_op jit(solution)/shard_map/all_gather | solution.py:8
  7.9 141.3 %all-gather.14.cloned.1.call-start = ((), (), s32[]{:S(2)}) async-start(), calls=%async_computation.5 | async-start | bytes 2162688 | tf_op jit(solution)/shard_map/all_gather | solution.py:36
  9.5 201.3 %all-gather.16.cloned.1.call-start = ((), (), s32[]{:S(2)}) async-start(), calls=%async_computation.6 | async-start | bytes 2162688 | tf_op jit(solution)/shard_map/all_gather | solution.py:41
  10.2 270.3 %all-gather.10.cloned.1.call-start = ((), (), s32[]{:S(2)}) async-start(), calls=%async_computation.2 | async-start | bytes 8650752 | tf_op jit(solution)/shard_map/all_gather | solution.py:30
  10.8 357.5 %all-gather.12.cloned.1.call-start = ((), (), s32[]{:S(2)}) async-start(), calls=%async_computation.3 | async-start | bytes 8650752 | tf_op jit(solution)/shard_map/all_gather | solution.py:76
  11.4 479.1 %reduce-scatter.2.cloned.1.call-start = ((), (), s32[]{:S(2)}) async-start(), calls=%async_computation.4 | async-start | bytes 2359296 | tf_op jit(solution)/shard_map/reduce_scatter | solution.py:83
  89.3 2.3 copy-start
  286.5 4.2 copy-start.1
Sparse Core Ops, SparseCore 0:
  10.6 78.6 all-gather.7
  91.8 57.4 all-gather.13
  151.7 59.0 all-gather.15
  212.5 68.0 all-gather.9
  282.2 86.1 all-gather.11
  397.4 93.0 reduce-scatter.1
where the time goes:
time: 499 us; the launch traced here: 497 us
  waiting for transfers between devices  415 us (83%)
  local copies, waits for them, and re-layouts  29.3 us (6%)
  matrix products  22.3 us (4%)
  other arithmetic  16.1 us (3%)
  between operations  14.3 us (3%)
    reduce_scatter x1, waiting for transfers between devices, on_device(): lax.psum_scatter(true_order.astype(jnp.bfloat16), 'tp', scatter_dimension...  92.6 us
    all_gather x1, waiting for transfers between devices, on_device(): lax.all_gather(wo_new, 'grp', axis=1, tiled=True)  76.7 us
    all_gather x1, waiting for transfers between devices, on_device(): gathered = lax.all_gather(states, 'tp', axis=2, tiled=True)  73.3 us
    all_gather x1, waiting for transfers between devices, on_device(): lax.all_gather(wq_new, 'grp', axis=0, tiled=True)  67.4 us
    all_gather x1, waiting for transfers between devices, on_device(): lax.all_gather(wkv_new[1], 'grp', axis=0, tiled=True)  59.2 us
    all_gather x1, waiting for transfers between devices, on_device(): lax.all_gather(wkv_new[0], 'grp', axis=0, tiled=True)  43.4 us
    dot_general x1, local copies, waits for them, and re-layouts, on_device(): jnp.dot(heads, lax.all_gather(wo_new, 'grp', axis=1, tiled=True), preferr...  11.9 us
  transfers between devices with their start and end apart: 6, of which 6 were waited for; matrix products, arithmetic and copies ran while one was open for 8% of the time, Pallas kernels for 0%

commit v1 on v0

v1 whole, which is shorter than its diff:
```python
import functools

import jax
import jax.numpy as jnp
from jax import lax
from jax.experimental import pallas as pl
from jax.experimental.pallas import tpu as pltpu
from jax.sharding import PartitionSpec as P

MESH = pl.DeviceIdType.MESH
F32 = jnp.float32
BF16 = jnp.bfloat16


def kernel(
    plan, lengths, states, cache, wq, wkv, wo,
    out, new_kv,
    own_q, own_kv,
    wa, wb, st, xn, acc, keys, values, lens, q8, h8, heads, kvn, inverse,
    part, from_left, from_right, transit, far_out, far_in,
    local_sem, st_send, st_recv, w_send, w_recv, r_send, r_recv,
):
    grp = lax.axis_index("grp")
    tp = lax.axis_index("tp")
    z, x, c = grp // 8, lax.rem(grp // 2, 4), lax.rem(grp, 2)
    y, zh = tp // 2, lax.rem(tp, 2)

    def mod4(v):
        return lax.rem(v + 4, 4)

    def block_of(z_, x_, c_):
        return (z_ * 4 + x_) * 2 + c_

    def device(x_=x, y_=y, z_=z, zh_=zh, c_=c):
        return (block_of(z_, x_, c_), y_ * 2 + zh_)

    xl, xr, xo = mod4(x - 1), mod4(x + 1), mod4(x + 2)
    yl, yr, yo = mod4(y - 1), mod4(y + 1), mod4(y + 2)
    zk = [z, z + 1 - 2 * lax.rem(z, 2), mod4(z + 2), 3 - z]

    locals_ = [
        pltpu.make_async_copy(wq, own_q, local_sem.at[0]),
        pltpu.make_async_copy(wkv.at[0], own_kv.at[0], local_sem.at[1]),
        pltpu.make_async_copy(wkv.at[1], own_kv.at[1], local_sem.at[2]),
        pltpu.make_async_copy(states, st.at[tp], local_sem.at[3]),
        pltpu.make_async_copy(wo, wb.at[grp], local_sem.at[4]),
        pltpu.make_async_copy(cache.at[0], keys, local_sem.at[5]),
        pltpu.make_async_copy(cache.at[1], values, local_sem.at[6]),
    ]
    for copy in locals_:
        copy.start()

    partners = [
        device(x_=xl), device(x_=xr), device(c_=1 - c),
        device(y_=yl), device(y_=yr), device(y_=yo), device(zh_=1 - zh),
        device(z_=zk[1]), device(z_=zk[2]), device(z_=zk[3]),
    ]
    barrier = pltpu.get_barrier_semaphore()
    for partner in partners:
        pl.semaphore_signal(barrier, inc=1, device_id=partner, device_id_type=MESH)
    for i in (0, 1, 2):
        locals_[i].wait()
    wa[grp, :, 0:512] = own_q[...]
    wa[grp, :, 512:640] = own_kv[0]
    wa[grp, :, 640:768] = own_kv[1]
    pl.semaphore_wait(barrier, len(partners))

    sent = []

    def send(src, dst, send_sem, recv_sem, to):
        copy = pltpu.make_async_remote_copy(
            src_ref=src, dst_ref=dst, send_sem=send_sem, recv_sem=recv_sem,
            device_id=to, device_id_type=MESH,
        )
        copy.start()
        sent.append(copy)

    def arrived(dst, recv_sem):
        pltpu.make_async_remote_copy(
            src_ref=dst, dst_ref=dst, send_sem=recv_sem, recv_sem=recv_sem,
            device_id=device(c_=1 - c), device_id_type=MESH,
        ).wait_recv()

    stores = (wa, wb)
    halves = (128, 256)

    def z_sends(t):
        for k in (1, 2, 3):
            ref = stores[t].at[grp]
            send(ref, ref, w_send.at[t, k - 1], w_recv.at[t, k - 1], device(z_=zk[k]))

    def base(k):
        return 3 + 8 * k

    def sibling(t, k, i, ref):
        s = base(k) + 4 + i
        send(ref, ref, w_send.at[t, s], w_recv.at[t, s], device(c_=1 - c))

    def e1(t, k):
        ref = stores[t].at[block_of(zk[k], x, c)]
        if k:
            arrived(ref, w_recv.at[t, k - 1])
        s = base(k)
        send(ref, ref, w_send.at[t, s], w_recv.at[t, s], device(x_=xr))
        send(ref, ref, w_send.at[t, s + 1], w_recv.at[t, s + 1], device(x_=xl))
        sibling(t, k, 0, ref)

    def e2(t, k):
        s = base(k)
        half = halves[t]
        bl = block_of(zk[k], xl, c)
        ref = stores[t].at[bl]
        arrived(ref, w_recv.at[t, s])
        low = stores[t].at[bl, pl.ds(0, half)]
        send(low, low, w_send.at[t, s + 2], w_recv.at[t, s + 2], device(x_=xr))
        sibling(t, k, 1, ref)
        br = block_of(zk[k], xr, c)
        ref = stores[t].at[br]
        arrived(ref, w_recv.at[t, s + 1])
        high = stores[t].at[br, pl.ds(half, half)]
        send(high, high, w_send.at[t, s + 3], w_recv.at[t, s + 3], device(x_=xl))
        sibling(t, k, 2, ref)

    def e3(t, k):
        s = base(k)
        half = halves[t]
        bo = block_of(zk[k], xo, c)
        arrived(stores[t].at[bo, pl.ds(0, half)], w_recv.at[t, s + 2])
        arrived(stores[t].at[bo, pl.ds(half, half)], w_recv.at[t, s + 3])
        sibling(t, k, 3, stores[t].at[bo])

    def e4(t, k):
        for i, x_ in enumerate((x, xl, xr, xo)):
            s = base(k) + 4 + i
            arrived(stores[t].at[block_of(zk[k], x_, 1 - c)], w_recv.at[t, s])

    tp_far = y * 2 + 1 - zh

    def spread_states(first, t):
        for i, y_ in enumerate((yr, yl, yo)):
            send(st.at[t], st.at[t], st_send.at[first + i], st_recv.at[first + i], device(y_=y_))

    e1(0, 0)
    z_sends(0)
    locals_[3].wait()
    send(st.at[tp], st.at[tp], st_send.at[0], st_recv.at[0], device(zh_=1 - zh))
    spread_states(1, tp)
    locals_[4].wait()
    z_sends(1)

    acc[...] = jnp.zeros_like(acc)

    def one_length(r, carry):
        lens[pl.ds(r, 1), :] = jnp.full((1, 128), lengths[r], jnp.int32)
        return carry

    lax.fori_loop(0, 64, one_length, 0)

    def one_inverse(tb, carry):
        def look(b, found):
            return jnp.maximum(found, jnp.where(plan[b] == tb, b, 0))

        inverse[tb] = lax.fori_loop(0, 32, look, jnp.int32(0), unroll=8)
        return carry

    lax.fori_loop(0, 32, one_inverse, 0)

    e2(0, 0)
    e1(0, 1)
    arrived(st.at[tp_far], st_recv.at[0])
    spread_states(4, tp_far)
    e1(0, 2)
    e3(0, 0)
    e2(0, 1)
    e1(0, 3)
    e3(0, 1)

    for first, zh_ in ((1, zh), (4, 1 - zh)):
        for i, y_ in enumerate((yl, yr, yo)):
            arrived(st.at[y_ * 2 + zh_], st_recv.at[first + i])

    def squares(t, total):
        wide = st[t].astype(F32)
        return total + jnp.sum(wide * wide, axis=-1, keepdims=True)

    total = lax.fori_loop(0, 8, squares, jnp.zeros((128, 1), F32))
    gain = lax.rsqrt(total / 8192.0 + 1e-05)

    def normalise(t, carry):
        for j in range(4):
            wide = st[t, :, 256 * j : 256 * (j + 1)].astype(F32)
            xn[t * 4 + j] = (wide * gain).astype(BF16)
        return carry

    lax.fori_loop(0, 8, normalise, 0)

    def project(k):

        def one(i, carry):
            b = zk[k] * 8 + i
            left = xn[plan[b]]
            acc[...] += jnp.dot(left, wa[b], preferred_element_type=F32)
            return carry

        lax.fori_loop(0, 8, one, 0)

    e2(0, 2)
    e1(1, 0)
    e3(0, 2)
    e2(0, 3)
    e1(1, 1)
    e3(0, 3)
    e1(1, 2)
    for k in range(4):
        e4(0, k)
    for k in range(4):
        project(k)

    for s in range(2):
        rows = slice(64 * s, 64 * (s + 1))
        for g in range(4):
            piece = acc[rows, 128 * g : 128 * (g + 1)]
            q8[:, 4 * s + g, :] = piece.astype(BF16).astype(F32)
        for i in range(2):
            piece = acc[rows, 512 + 128 * i : 640 + 128 * i].astype(BF16)
            new_kv[s, i] = piece
            kvn[s, i] = piece.astype(F32)
    locals_[5].wait()
    locals_[6].wait()
    scale = 1.0 / 128**0.5

    def attend(n):
        rows = pl.ds(16 * n, 16)
        q = q8[rows]
        score = lax.dot_general(
            q.astype(BF16), keys[rows], (((2,), (2,)), ((0,), (0,))), preferred_element_type=F32
        ) * scale
        slots = lax.broadcasted_iota(jnp.int32, (16, 8, 128), 2)
        score = jnp.where(slots < lens[rows][:, None, :], score, -1e30)
        own = [
            jnp.sum(q * kvn[t, 0, rows][:, None, :], axis=-1, keepdims=True) * scale
            for t in range(2)
        ]
        second = lax.broadcasted_iota(jnp.int32, (16, 8, 1), 1) >= 4
        own[1] = jnp.where(second, own[1], -1e30)
        top = jnp.maximum(jnp.max(score, axis=-1, keepdims=True), jnp.maximum(own[0], own[1]))
        cached = jnp.exp(score - top)
        fresh = [jnp.exp(o - top) for o in own]
        total = jnp.sum(cached, axis=-1, keepdims=True) + fresh[0] + fresh[1]
        weight = (cached / total).astype(BF16)
        result = lax.dot_general(
            weight, values[rows], (((2,), (1,)), ((0,), (0,))), preferred_element_type=F32
        )
        for t in range(2):
            w = (fresh[t] / total).astype(BF16).astype(F32)
            result = result + w * kvn[t, 1, rows][:, None, :]
        h8[rows] = result

    attend(0)
    attend(1)
    e2(1, 0)
    e1(1, 3)
    attend(2)
    attend(3)
    e3(1, 0)
    for s in range(2):
        for g in range(4):
            heads[64 * s : 64 * (s + 1), 128 * g : 128 * (g + 1)] = h8[:, 4 * s + g, :].astype(BF16)
    e2(1, 1)
    e3(1, 1)
    e2(1, 2)
    e3(1, 2)
    e2(1, 3)
    e3(1, 3)
    for k in range(4):
        e4(1, k)

    def product(j, t):
        right = wb[inverse[t * 4 + j]]
        part[j, t] = jnp.dot(heads[...], right, preferred_element_type=F32).astype(BF16)

    def r_send_to(j, i, src, dst, to):
        send(src, dst, r_send.at[j, i], r_recv.at[j, i], to)

    to_left, to_right = device(y_=yl), device(y_=yr)
    for j in range(4):
        product(j, yo * 2)
        r_send_to(j, 0, part.at[j, yo * 2], transit.at[j, 0], to_right)
        product(j, yo * 2 + 1)
        r_send_to(j, 1, part.at[j, yo * 2 + 1], transit.at[j, 1], to_left)
        product(j, yr * 2 + 1)
        r_send_to(j, 2, part.at[j, yr * 2 + 1], from_left.at[j, 1], to_right)
        product(j, yl * 2)
        r_send_to(j, 3, part.at[j, yl * 2], from_right.at[j, 0], to_left)
        product(j, yr * 2)
        product(j, yl * 2 + 1)
        product(j, y * 2)
        product(j, y * 2 + 1)

    def add(j, t, i):
        part[j, t] = (part[j, t].astype(F32) + transit[j, i].astype(F32)).astype(BF16)

    for j in range(4):
        arrived(transit.at[j, 0], r_recv.at[j, 0])
        add(j, yr * 2, 0)
        r_send_to(j, 4, part.at[j, yr * 2], from_left.at[j, 0], to_right)
        arrived(transit.at[j, 1], r_recv.at[j, 1])
        add(j, yl * 2 + 1, 1)
        r_send_to(j, 5, part.at[j, yl * 2 + 1], from_right.at[j, 1], to_left)

    def summed(j, h):
        return (
            part[j, y * 2 + h].astype(F32) + from_left[j, h].astype(F32) + from_right[j, h].astype(F32)
        )

    for j in range(4):
        arrived(from_left.at[j, 1], r_recv.at[j, 2])
        arrived(from_right.at[j, 0], r_recv.at[j, 3])
        arrived(from_left.at[j, 0], r_recv.at[j, 4])
        arrived(from_right.at[j, 1], r_recv.at[j, 5])
        far_out[j] = summed(j, 1 - zh).astype(BF16)
        r_send_to(j, 6, far_out.at[j], far_in.at[j], device(zh_=1 - zh))
    for j in range(4):
        arrived(far_in.at[j], r_recv.at[j, 6])
        out[:, 256 * j : 256 * (j + 1)] = (summed(j, zh) + far_in[j].astype(F32)).astype(BF16)

    for copy in sent:
        copy.wait_send()


def on_device(states, cache, lengths, plan, wq_new, wkv_new, wo_new):
    vmem = pltpu.VMEM
    dma = pltpu.SemaphoreType.DMA
    hbm = pl.BlockSpec(memory_space=pltpu.HBM)
    smem = pl.BlockSpec(memory_space=pltpu.SMEM)
    attended, new_kv = pl.pallas_call(
        kernel,
        out_shape=(
            jax.ShapeDtypeStruct((128, 1024), BF16),
            jax.ShapeDtypeStruct((2, 2, 64, 128), BF16),
        ),
        in_specs=[smem, smem, hbm, hbm, hbm, hbm, hbm],
        out_specs=[pl.BlockSpec(memory_space=pltpu.VMEM)] * 2,
        scratch_shapes=[
            vmem((256, 512), BF16),
            vmem((2, 256, 128), BF16),
            vmem((32, 256, 768), BF16),
            vmem((32, 512, 256), BF16),
            vmem((8, 128, 1024), BF16),
            vmem((32, 128, 256), BF16),
            vmem((128, 768), F32),
            vmem((64, 128, 128), BF16),
            vmem((64, 128, 128), BF16),
            vmem((64, 128), jnp.int32),
            vmem((64, 8, 128), F32),
            vmem((64, 8, 128), F32),
            vmem((128, 512), BF16),
            vmem((2, 2, 64, 128), F32),
            pltpu.SMEM((32,), jnp.int32),
            vmem((4, 8, 128, 256), BF16),
            vmem((4, 2, 128, 256), BF16),
            vmem((4, 2, 128, 256), BF16),
            vmem((4, 2, 128, 256), BF16),
            vmem((4, 128, 256), BF16),
            vmem((4, 128, 256), BF16),
            dma((7,)),
            dma((7,)), dma((7,)),
            dma((2, 35)), dma((2, 35)),
            dma((4, 7)), dma((4, 7)),
        ],
        compiler_params=pltpu.CompilerParams(
            collective_id=0, has_side_effects=True, vmem_limit_bytes=60 * 2**20
        ),
        name="layer",
    )(
        plan, lengths, states.reshape(128, 1024), cache.reshape(2, 64, 128, 128),
        wq_new, wkv_new, wo_new,
    )
    return attended.reshape(2, 64, 1024), new_kv.reshape(2, 2, 64, 1, 128)


def solution(mesh):
    return jax.shard_map(
        on_device,
        mesh=mesh,
        in_specs=(
            P(None, "grp", "tp"),
            P(None, "grp", "tp", None, None),
            P("grp"),
            P(),
            P("grp", "tp"),
            P(None, "grp", "tp"),
            P("tp", "grp"),
        ),
        out_specs=(P(None, "grp", "tp"), P(None, None, "grp", "tp", None)),
        check_vma=False,
    )
```

time: 499 us -> 161 us (0.32)
  the two profiles are of different devices: /device:TPU:1 before, /device:TPU:33 now
where the time goes in v1:
time: 161 us
  Pallas kernels  157 us (98%)
  local copies, waits for them, and re-layouts  3.14 us (2%)
    pallas_call x1, Pallas kernels, on_device(): pl.pallas_call(kernel, out_shape=(jax.ShapeDtypeStruct((128, 1024), BF16)...  157 us

profile of v1, /device:TPU:33, one launch (start us, length us, event | category | flops | bytes accessed | tf_op | source)
XLA Modules:
  0.0 161.2 jit_solution(10076794705379417738)
XLA Ops:
  0.6 157.5 %layer.1 = (bf16[128,1024]{1,0:T(8,128)(2,1)}, bf16[2,2,64,128]{3,2,1,0:T(8,128)(2,1)}) custom-call(s32[32]{0:T(128)} %plan.1, s32[64]{0:T(128)} %lengths.1, bf16[128,1024]{1,0:T(8,128)(2,1)} %bitcast.7, bf16[2,64,128,128]{3,2,1,0:T(8,128)(2,1)} %bitcast.6, bf16[256,512]{1,0:T(8,128)(2,1)} %wq.1, bf16[2,256,128]{2,1,0:T(8,128)(2,1)} %wkv.1, bf16[512,256]{1,0:T(8,128)(2,1)} %wo.1), custom_call_target="tpu_custom_call" | custom-call | tf_op jit(solution)/shard_map/layer/pallas_call | solution.py:336
  158.1 1.7 %copy.12 = bf16[2,64,1024]{2,1,0:T(8,128)(2,1)} copy(bf16[2,64,1024]{2,1,0:T(8,128)(2,1)} %bitcast.8) | data formatting | bytes 524288
  159.8 1.5 copy.13

commit v2 on v1

--- a/solution.py
+++ b/solution.py
@@ -18,7 +18,7 @@
     own_q, own_kv,
     wa, wb, st, xn, acc, keys, values, lens, q8, h8, heads, kvn, inverse,
     part, from_left, from_right, transit, far_out, far_in,
-    local_sem, st_send, st_recv, w_send, w_recv, r_send, r_recv,
+    local_sem, st_send, st_recv, w_send, w_recv, z_send, r_send, r_recv,
 ):
     grp = lax.axis_index("grp")
     tp = lax.axis_index("tp")
@@ -36,7 +36,10 @@
 
     xl, xr, xo = mod4(x - 1), mod4(x + 1), mod4(x + 2)
     yl, yr, yo = mod4(y - 1), mod4(y + 1), mod4(y + 2)
-    zk = [z, z + 1 - 2 * lax.rem(z, 2), mod4(z + 2), 3 - z]
+    z_pair, z_mirror = z + 1 - 2 * lax.rem(z, 2), 3 - z
+    upper = z // 2
+    inner = lax.rem(z + 1, 4) // 2 == 1
+    zk = [z, z_pair, 2 - upper, 3 - 3 * upper]
 
     locals_ = [
         pltpu.make_async_copy(wq, own_q, local_sem.at[0]),
@@ -53,7 +56,7 @@
     partners = [
         device(x_=xl), device(x_=xr), device(c_=1 - c),
         device(y_=yl), device(y_=yr), device(y_=yo), device(zh_=1 - zh),
-        device(z_=zk[1]), device(z_=zk[2]), device(z_=zk[3]),
+        device(z_=z_pair), device(z_=z_mirror),
     ]
     barrier = pltpu.get_barrier_semaphore()
     for partner in partners:
@@ -84,10 +87,27 @@
     stores = (wa, wb)
     halves = (128, 256)
 
-    def z_sends(t):
-        for k in (1, 2, 3):
-            ref = stores[t].at[grp]
-            send(ref, ref, w_send.at[t, k - 1], w_recv.at[t, k - 1], device(z_=zk[k]))
+    inner_sent = []
+
+    def z_start(t):
+        ref = stores[t].at[grp]
+        send(ref, ref, w_send.at[t, 0], w_recv.at[t, 0], device(z_=z_pair))
+        z_cross(t, 0)
+
+    def z_cross(t, k):
+        ref = stores[t].at[block_of(zk[k], x, c)]
+        to = device(z_=z_mirror) if k < 2 else device(z_=z_pair)
+        arrives = 1 + k if k < 2 else k - 1
+        copy = pltpu.make_async_remote_copy(
+            src_ref=ref, dst_ref=ref, send_sem=z_send.at[t, k], recv_sem=w_recv.at[t, arrives],
+            device_id=to, device_id_type=MESH,
+        )
+        pl.when(inner)(copy.start)
+        inner_sent.append(copy)
+
+    def z_next(t, k):
+        arrived(stores[t].at[block_of(zk[k], x, c)], w_recv.at[t, k - 1])
+        z_cross(t, k)
 
     def base(k):
         return 3 + 8 * k
@@ -98,8 +118,6 @@
 
     def e1(t, k):
         ref = stores[t].at[block_of(zk[k], x, c)]
-        if k:
-            arrived(ref, w_recv.at[t, k - 1])
         s = base(k)
         send(ref, ref, w_send.at[t, s], w_recv.at[t, s], device(x_=xr))
         send(ref, ref, w_send.at[t, s + 1], w_recv.at[t, s + 1], device(x_=xl))
@@ -141,12 +159,9 @@
             send(st.at[t], st.at[t], st_send.at[first + i], st_recv.at[first + i], device(y_=y_))
 
     e1(0, 0)
-    z_sends(0)
+    z_start(0)
     locals_[3].wait()
-    send(st.at[tp], st.at[tp], st_send.at[0], st_recv.at[0], device(zh_=1 - zh))
     spread_states(1, tp)
-    locals_[4].wait()
-    z_sends(1)
 
     acc[...] = jnp.zeros_like(acc)
 
@@ -165,15 +180,27 @@
 
     lax.fori_loop(0, 32, one_inverse, 0)
 
+    z_next(0, 1)
+    e1(0, 1)
     e2(0, 0)
-    e1(0, 1)
+    z_next(0, 2)
+    e1(0, 2)
+    send(st.at[tp], st.at[tp], st_send.at[0], st_recv.at[0], device(zh_=1 - zh))
+    e3(0, 0)
+    z_next(0, 3)
+    e2(0, 1)
+    e1(0, 3)
+    locals_[4].wait()
+    z_start(1)
     arrived(st.at[tp_far], st_recv.at[0])
     spread_states(4, tp_far)
-    e1(0, 2)
-    e3(0, 0)
-    e2(0, 1)
-    e1(0, 3)
     e3(0, 1)
+    z_next(1, 1)
+    e2(0, 2)
+    e1(1, 0)
+    z_next(1, 2)
+    e3(0, 2)
+    z_next(1, 3)
 
     for first, zh_ in ((1, zh), (4, 1 - zh)):
         for i, y_ in enumerate((yl, yr, yo)):
@@ -204,13 +231,12 @@
 
         lax.fori_loop(0, 8, one, 0)
 
-    e2(0, 2)
-    e1(1, 0)
-    e3(0, 2)
     e2(0, 3)
     e1(1, 1)
     e3(0, 3)
     e1(1, 2)
+    e2(1, 0)
+    e1(1, 3)
     for k in range(4):
         e4(0, k)
     for k in range(4):
@@ -258,15 +284,13 @@
 
     attend(0)
     attend(1)
-    e2(1, 0)
-    e1(1, 3)
+    e2(1, 1)
     attend(2)
     attend(3)
     e3(1, 0)
     for s in range(2):
         for g in range(4):
             heads[64 * s : 64 * (s + 1), 128 * g : 128 * (g + 1)] = h8[:, 4 * s + g, :].astype(BF16)
-    e2(1, 1)
     e3(1, 1)
     e2(1, 2)
     e3(1, 2)
@@ -326,6 +350,11 @@
 
     for copy in sent:
         copy.wait_send()
+
+    @pl.when(inner)
+    def _():
+        for copy in inner_sent:
+            copy.wait_send()
 
 
 def on_device(states, cache, lengths, plan, wq_new, wkv_new, wo_new):
@@ -365,7 +394,7 @@
             vmem((4, 128, 256), BF16),
             dma((7,)),
             dma((7,)), dma((7,)),
-            dma((2, 35)), dma((2, 35)),
+            dma((2, 35)), dma((2, 35)), dma((2, 4)),
             dma((4, 7)), dma((4, 7)),
         ],
         compiler_params=pltpu.CompilerParams(

time: 161 us -> 144 us (0.89)
  the two profiles are of different devices: /device:TPU:33 before, /device:TPU:1 now
where the time goes in v2:
time: 144 us; the launch traced here: 143 us
  Pallas kernels  140 us (97%)
  local copies, waits for them, and re-layouts  3.14 us (2%)
    pallas_call x1, Pallas kernels, on_device(): pl.pallas_call(kernel, out_shape=(jax.ShapeDtypeStruct((128, 1024), BF16)...  140 us
    unnamed x2, local copies, waits for them, and re-layouts  3.14 us

profile of v2, /device:TPU:1, one launch (start us, length us, event | category | flops | bytes accessed | tf_op | source)
XLA Modules:
  0.0 143.5 jit_solution(3454858145562707379)
XLA Ops:
  0.6 139.7 %layer.1 = (bf16[128,1024]{1,0:T(8,128)(2,1)}, bf16[2,2,64,128]{3,2,1,0:T(8,128)(2,1)}) custom-call(s32[32]{0:T(128)} %plan.1, s32[64]{0:T(128)} %lengths.1, bf16[128,1024]{1,0:T(8,128)(2,1)} %bitcast.7, bf16[2,64,128,128]{3,2,1,0:T(8,128)(2,1)} %bitcast.6, bf16[256,512]{1,0:T(8,128)(2,1)} %wq.1, bf16[2,256,128]{2,1,0:T(8,128)(2,1)} %wkv.1, bf16[512,256]{1,0:T(8,128)(2,1)} %wo.1), custom_call_target="tpu_custom_call" | custom-call | tf_op jit(solution)/shard_map/layer/pallas_call | solution.py:365
  140.4 1.7 %copy.12 = bf16[2,64,1024]{2,1,0:T(8,128)(2,1)} copy(bf16[2,64,1024]{2,1,0:T(8,128)(2,1)} %bitcast.8) | data formatting | bytes 524288
  142.0 1.5 %copy.13 = bf16[2,2,64,1,128]{4,2,3,1,0:T(8,128)(2,1)} copy(bf16[2,2,64,1,128]{4,2,3,1,0:T(8,128)(2,1)} %bitcast.9) | data formatting | bytes 131072

commit v3 on v1

--- a/solution.py
+++ b/solution.py
@@ -8,6 +8,8 @@
 from jax.sharding import PartitionSpec as P
 
 MESH = pl.DeviceIdType.MESH
+FIRST = 192
+REST = 512 - FIRST
 F32 = jnp.float32
 BF16 = jnp.bfloat16
 
@@ -16,9 +18,9 @@
     plan, lengths, states, cache, wq, wkv, wo,
     out, new_kv,
     own_q, own_kv,
-    wa, wb, st, xn, acc, keys, values, lens, q8, h8, heads, kvn, inverse,
+    wa0, wa1, wa2, wa3, wb, wc, st, xn, xp, acc, keys, values, lens, q8, h8, heads, kvn, inverse,
     part, from_left, from_right, transit, far_out, far_in,
-    local_sem, st_send, st_recv, w_send, w_recv, r_send, r_recv,
+    local_sem, st_send, st_recv, w_send, w_recv, z_send, c_send, c_recv, cz_send, r_send, r_recv,
 ):
     grp = lax.axis_index("grp")
     tp = lax.axis_index("tp")
@@ -36,16 +38,20 @@
 
     xl, xr, xo = mod4(x - 1), mod4(x + 1), mod4(x + 2)
     yl, yr, yo = mod4(y - 1), mod4(y + 1), mod4(y + 2)
-    zk = [z, z + 1 - 2 * lax.rem(z, 2), mod4(z + 2), 3 - z]
+    z_pair, z_mirror = z + 1 - 2 * lax.rem(z, 2), 3 - z
+    upper = z // 2
+    inner = lax.rem(z + 1, 4) // 2 == 1
+    zk = [z, z_pair, 2 - upper, 3 - 3 * upper]
 
     locals_ = [
         pltpu.make_async_copy(wq, own_q, local_sem.at[0]),
         pltpu.make_async_copy(wkv.at[0], own_kv.at[0], local_sem.at[1]),
         pltpu.make_async_copy(wkv.at[1], own_kv.at[1], local_sem.at[2]),
         pltpu.make_async_copy(states, st.at[tp], local_sem.at[3]),
-        pltpu.make_async_copy(wo, wb.at[grp], local_sem.at[4]),
+        pltpu.make_async_copy(wo.at[pl.ds(FIRST, REST)], wb.at[grp], local_sem.at[4]),
         pltpu.make_async_copy(cache.at[0], keys, local_sem.at[5]),
         pltpu.make_async_copy(cache.at[1], values, local_sem.at[6]),
+        pltpu.make_async_copy(wo.at[pl.ds(0, FIRST)], wc.at[c * 16 + z * 4 + x], local_sem.at[7]),
     ]
     for copy in locals_:
         copy.start()
@@ -53,16 +59,17 @@
     partners = [
         device(x_=xl), device(x_=xr), device(c_=1 - c),
         device(y_=yl), device(y_=yr), device(y_=yo), device(zh_=1 - zh),
-        device(z_=zk[1]), device(z_=zk[2]), device(z_=zk[3]),
+        device(z_=z_pair), device(z_=z_mirror),
     ]
     barrier = pltpu.get_barrier_semaphore()
     for partner in partners:
         pl.semaphore_signal(barrier, inc=1, device_id=partner, device_id_type=MESH)
     for i in (0, 1, 2):
         locals_[i].wait()
-    wa[grp, :, 0:512] = own_q[...]
-    wa[grp, :, 512:640] = own_kv[0]
-    wa[grp, :, 640:768] = own_kv[1]
+    mine = x * 2 + c
+    wa0[mine, :, 0:512] = own_q[...]
+    wa0[mine, :, 512:640] = own_kv[0]
+    wa0[mine, :, 640:768] = own_kv[1]
     pl.semaphore_wait(barrier, len(partners))
 
     sent = []
@@ -81,13 +88,37 @@
             device_id=device(c_=1 - c), device_id_type=MESH,
         ).wait_recv()
 
-    stores = (wa, wb)
-    halves = (128, 256)
-
-    def z_sends(t):
-        for k in (1, 2, 3):
-            ref = stores[t].at[grp]
-            send(ref, ref, w_send.at[t, k - 1], w_recv.at[t, k - 1], device(z_=zk[k]))
+    wa = (wa0, wa1, wa2, wa3)
+
+    def held(t, k, x_, c_, there=None):
+        if t == 0:
+            return wa[k if there is None else there].at[x_ * 2 + c_]
+        return wb.at[block_of(zk[k], x_, c_)]
+
+    halves = (128, REST // 2)
+
+    def z_start(t):
+        send(held(t, 0, x, c), held(t, 0, x, c, 1), w_send.at[t, 0], w_recv.at[t, 0], device(z_=z_pair))
+        pl.when(inner)(lambda: z_copy(t, 0).start())
+
+    def z_copy(t, k):
+        there = k + 2 if k < 2 else k
+        return pltpu.make_async_remote_copy(
+            src_ref=held(t, k, x, c), dst_ref=held(t, k, x, c, there),
+            send_sem=z_send.at[t, k], recv_sem=w_recv.at[t, there - 1],
+            device_id=device(z_=z_mirror) if k < 2 else device(z_=z_pair), device_id_type=MESH,
+        )
+
+    def z_in(t, k):
+        @pl.when(inner)
+        def _():
+            arrived(held(t, k, x, c), w_recv.at[t, k - 1])
+            z_copy(t, k).start()
+
+    def z_out(t, k):
+        @pl.when(jnp.logical_not(inner))
+        def _():
+            arrived(held(t, k, x, c), w_recv.at[t, k - 1])
 
     def base(k):
         return 3 + 8 * k
@@ -97,9 +128,7 @@
         send(ref, ref, w_send.at[t, s], w_recv.at[t, s], device(c_=1 - c))
 
     def e1(t, k):
-        ref = stores[t].at[block_of(zk[k], x, c)]
-        if k:
-            arrived(ref, w_recv.at[t, k - 1])
+        ref = held(t, k, x, c)
         s = base(k)
         send(ref, ref, w_send.at[t, s], w_recv.at[t, s], device(x_=xr))
         send(ref, ref, w_send.at[t, s + 1], w_recv.at[t, s + 1], device(x_=xl))
@@ -108,31 +137,80 @@
     def e2(t, k):
         s = base(k)
         half = halves[t]
-        bl = block_of(zk[k], xl, c)
-        ref = stores[t].at[bl]
-        arrived(ref, w_recv.at[t, s])
-        low = stores[t].at[bl, pl.ds(0, half)]
-        send(low, low, w_send.at[t, s + 2], w_recv.at[t, s + 2], device(x_=xr))
-        sibling(t, k, 1, ref)
-        br = block_of(zk[k], xr, c)
-        ref = stores[t].at[br]
-        arrived(ref, w_recv.at[t, s + 1])
-        high = stores[t].at[br, pl.ds(half, half)]
-        send(high, high, w_send.at[t, s + 3], w_recv.at[t, s + 3], device(x_=xl))
-        sibling(t, k, 2, ref)
+        for i, x_, to, rows in ((0, xl, xr, pl.ds(0, half)), (1, xr, xl, pl.ds(half, half))):
+            ref = held(t, k, x_, c)
+            arrived(ref, w_recv.at[t, s + i])
+            part_ref = ref.at[rows]
+            send(part_ref, part_ref, w_send.at[t, s + 2 + i], w_recv.at[t, s + 2 + i], device(x_=to))
+            sibling(t, k, 1 + i, ref)
 
     def e3(t, k):
         s = base(k)
         half = halves[t]
-        bo = block_of(zk[k], xo, c)
-        arrived(stores[t].at[bo, pl.ds(0, half)], w_recv.at[t, s + 2])
-        arrived(stores[t].at[bo, pl.ds(half, half)], w_recv.at[t, s + 3])
-        sibling(t, k, 3, stores[t].at[bo])
+        ref = held(t, k, xo, c)
+        arrived(ref.at[pl.ds(0, half)], w_recv.at[t, s + 2])
+        arrived(ref.at[pl.ds(half, half)], w_recv.at[t, s + 3])
+        sibling(t, k, 3, ref)
 
     def e4(t, k):
         for i, x_ in enumerate((x, xl, xr, xo)):
-            s = base(k) + 4 + i
-            arrived(stores[t].at[block_of(zk[k], x_, 1 - c)], w_recv.at[t, s])
+            arrived(held(t, k, x_, 1 - c), w_recv.at[t, base(k) + 4 + i])
+
+    def first_of(z_, x_, c_):
+        return c_ * 16 + z_ * 4 + x_
+
+    def first_row(k, c_):
+        return wc.at[pl.ds(first_of(zk[k], 0, c_), 4)]
+
+    def c1():
+        ref = wc.at[first_of(z, x, c)]
+        send(ref, ref, c_send.at[0], c_recv.at[0], device(x_=xr))
+        send(ref, ref, c_send.at[1], c_recv.at[1], device(x_=xl))
+
+    def c2():
+        half = FIRST // 2
+        for i, x_, to, rows in ((0, xl, xr, pl.ds(0, half)), (1, xr, xl, pl.ds(half, half))):
+            n = first_of(z, x_, c)
+            arrived(wc.at[n], c_recv.at[i])
+            ref = wc.at[n, rows]
+            send(ref, ref, c_send.at[2 + i], c_recv.at[2 + i], device(x_=to))
+
+    def c_copy(k):
+        ref = first_row(k, c)
+        arrives = 5 + k if k < 2 else 3 + k
+        return pltpu.make_async_remote_copy(
+            src_ref=ref, dst_ref=ref, send_sem=cz_send.at[k], recv_sem=c_recv.at[arrives],
+            device_id=device(z_=z_mirror) if k < 2 else device(z_=z_pair), device_id_type=MESH,
+        )
+
+    def c_sibling(k):
+        ref = first_row(k, c)
+        send(ref, ref, c_send.at[7 + k], c_recv.at[7 + k], device(c_=1 - c))
+
+    def c3():
+        half = FIRST // 2
+        n = first_of(z, xo, c)
+        arrived(wc.at[n, pl.ds(0, half)], c_recv.at[2])
+        arrived(wc.at[n, pl.ds(half, half)], c_recv.at[3])
+        ref = first_row(0, c)
+        send(ref, ref, c_send.at[4], c_recv.at[4], device(z_=z_pair))
+        pl.when(inner)(lambda: c_copy(0).start())
+        c_sibling(0)
+
+    def c_in(k):
+        @pl.when(inner)
+        def _():
+            arrived(first_row(k, c), c_recv.at[3 + k])
+            c_copy(k).start()
+
+    def c_out(k):
+        @pl.when(jnp.logical_not(inner))
+        def _():
+            arrived(first_row(k, c), c_recv.at[3 + k])
+
+    def c4():
+        for k in range(4):
+            arrived(first_row(k, 1 - c), c_recv.at[7 + k])
 
     tp_far = y * 2 + 1 - zh
 
@@ -141,14 +219,15 @@
             send(st.at[t], st.at[t], st_send.at[first + i], st_recv.at[first + i], device(y_=y_))
 
     e1(0, 0)
-    z_sends(0)
     locals_[3].wait()
     send(st.at[tp], st.at[tp], st_send.at[0], st_recv.at[0], device(zh_=1 - zh))
+    z_start(0)
     spread_states(1, tp)
+    locals_[7].wait()
+    c1()
     locals_[4].wait()
-    z_sends(1)
-
-    acc[...] = jnp.zeros_like(acc)
+    e1(1, 0)
+
 
     def one_length(r, carry):
         lens[pl.ds(r, 1), :] = jnp.full((1, 128), lengths[r], jnp.int32)
@@ -160,20 +239,39 @@
         def look(b, found):
             return jnp.maximum(found, jnp.where(plan[b] == tb, b, 0))
 
-        inverse[tb] = lax.fori_loop(0, 32, look, jnp.int32(0), unroll=8)
+        inverse[tb] = lax.fori_loop(0, 32, look, jnp.int32(0), unroll=32)
         return carry
 
-    lax.fori_loop(0, 32, one_inverse, 0)
+    def some_inverse(n):
+        lax.fori_loop(8 * n, 8 * n + 8, one_inverse, 0)
 
     e2(0, 0)
+    c2()
+    e2(1, 0)
+    z_in(0, 1)
+    z_in(0, 2)
+    z_out(0, 1)
     e1(0, 1)
     arrived(st.at[tp_far], st_recv.at[0])
     spread_states(4, tp_far)
+    e3(0, 0)
+    e3(1, 0)
+    z_in(0, 3)
+    z_out(0, 2)
     e1(0, 2)
-    e3(0, 0)
     e2(0, 1)
+    e3(0, 1)
+    z_out(0, 3)
+    z_start(1)
     e1(0, 3)
-    e3(0, 1)
+    z_in(1, 1)
+    z_in(1, 2)
+    e2(0, 2)
+    z_in(1, 3)
+    c3()
+    z_out(1, 1)
+    e1(1, 1)
+    e3(0, 2)
 
     for first, zh_ in ((1, zh), (4, 1 - zh)):
         for i, y_ in enumerate((yl, yr, yo)):
@@ -193,28 +291,32 @@
         return carry
 
     lax.fori_loop(0, 8, normalise, 0)
+    for k in range(4):
+        for i in range(8):
+            xp[k, :, 256 * i : 256 * (i + 1)] = xn[plan[zk[k] * 8 + i]]
 
     def project(k):
-
-        def one(i, carry):
-            b = zk[k] * 8 + i
-            left = xn[plan[b]]
-            acc[...] += jnp.dot(left, wa[b], preferred_element_type=F32)
-            return carry
-
-        lax.fori_loop(0, 8, one, 0)
-
-    e2(0, 2)
-    e1(1, 0)
-    e3(0, 2)
+        e4(0, k)
+        for n in range(3):
+            cols = slice(256 * n, 256 * (n + 1))
+            right = wa[k][:, :, cols].reshape(2048, 256)
+            sums = jnp.dot(xp[k], right, preferred_element_type=F32)
+            acc[:, cols] = sums if k == 0 else acc[:, cols] + sums
+
+    project(0)
+    project(1)
+    z_out(1, 2)
+    e1(1, 2)
+    project(2)
+    c_in(1)
+    c_in(2)
     e2(0, 3)
-    e1(1, 1)
+    z_out(1, 3)
+    e1(1, 3)
+    c_out(1)
+    c_sibling(1)
     e3(0, 3)
-    e1(1, 2)
-    for k in range(4):
-        e4(0, k)
-    for k in range(4):
-        project(k)
+    project(3)
 
     for s in range(2):
         rows = slice(64 * s, 64 * (s + 1))
@@ -256,34 +358,44 @@
             result = result + w * kvn[t, 1, rows][:, None, :]
         h8[rows] = result
 
+    e2(1, 1)
     attend(0)
     attend(1)
-    e2(1, 0)
-    e1(1, 3)
+    c_in(3)
     attend(2)
+    e3(1, 1)
+    c_out(2)
+    c_sibling(2)
     attend(3)
-    e3(1, 0)
+    e2(1, 2)
     for s in range(2):
         for g in range(4):
             heads[64 * s : 64 * (s + 1), 128 * g : 128 * (g + 1)] = h8[:, 4 * s + g, :].astype(BF16)
-    e2(1, 1)
-    e3(1, 1)
-    e2(1, 2)
+    some_inverse(0)
+    some_inverse(1)
     e3(1, 2)
+    some_inverse(2)
+    some_inverse(3)
     e2(1, 3)
+    c_out(3)
+    c_sibling(3)
     e3(1, 3)
     for k in range(4):
         e4(1, k)
+    c4()
 
     def product(j, t):
-        right = wb[inverse[t * 4 + j]]
-        part[j, t] = jnp.dot(heads[...], right, preferred_element_type=F32).astype(BF16)
+        b = inverse[t * 4 + j]
+        low = jnp.dot(heads[:, :FIRST], wc[lax.rem(b, 2) * 16 + b // 2], preferred_element_type=F32)
+        high = jnp.dot(heads[:, FIRST:], wb[b], preferred_element_type=F32)
+        part[j, t] = (low + high).astype(BF16)
 
     def r_send_to(j, i, src, dst, to):
         send(src, dst, r_send.at[j, i], r_recv.at[j, i], to)
 
     to_left, to_right = device(y_=yl), device(y_=yr)
-    for j in range(4):
+
+    def r1(j):
         product(j, yo * 2)
         r_send_to(j, 0, part.at[j, yo * 2], transit.at[j, 0], to_right)
         product(j, yo * 2 + 1)
@@ -300,7 +412,7 @@
     def add(j, t, i):
         part[j, t] = (part[j, t].astype(F32) + transit[j, i].astype(F32)).astype(BF16)
 
-    for j in range(4):
+    def r2(j):
         arrived(transit.at[j, 0], r_recv.at[j, 0])
         add(j, yr * 2, 0)
         r_send_to(j, 4, part.at[j, yr * 2], from_left.at[j, 0], to_right)
@@ -313,19 +425,39 @@
             part[j, y * 2 + h].astype(F32) + from_left[j, h].astype(F32) + from_right[j, h].astype(F32)
         )
 
-    for j in range(4):
+    def r3(j):
         arrived(from_left.at[j, 1], r_recv.at[j, 2])
         arrived(from_right.at[j, 0], r_recv.at[j, 3])
         arrived(from_left.at[j, 0], r_recv.at[j, 4])
         arrived(from_right.at[j, 1], r_recv.at[j, 5])
         far_out[j] = summed(j, 1 - zh).astype(BF16)
         r_send_to(j, 6, far_out.at[j], far_in.at[j], device(zh_=1 - zh))
+
+    r1(0)
+    r1(1)
+    r2(0)
+    r1(2)
+    r2(1)
+    r3(0)
+    r1(3)
+    r2(2)
+    r3(1)
+    r2(3)
+    r3(2)
+    r3(3)
     for j in range(4):
         arrived(far_in.at[j], r_recv.at[j, 6])
         out[:, 256 * j : 256 * (j + 1)] = (summed(j, zh) + far_in[j].astype(F32)).astype(BF16)
 
     for copy in sent:
         copy.wait_send()
+
+    @pl.when(inner)
+    def _():
+        for k in range(4):
+            for t in range(2):
+                z_copy(t, k).wait_send()
+            c_copy(k).wait_send()
 
 
 def on_device(states, cache, lengths, plan, wq_new, wkv_new, wo_new):
@@ -344,10 +476,12 @@
         scratch_shapes=[
             vmem((256, 512), BF16),
             vmem((2, 256, 128), BF16),
-            vmem((32, 256, 768), BF16),
-            vmem((32, 512, 256), BF16),
+            *[vmem((8, 256, 768), BF16)] * 4,
+            vmem((32, REST, 256), BF16),
+            vmem((32, FIRST, 256), BF16),
             vmem((8, 128, 1024), BF16),
             vmem((32, 128, 256), BF16),
+            vmem((4, 128, 2048), BF16),
             vmem((128, 768), F32),
             vmem((64, 128, 128), BF16),
             vmem((64, 128, 128), BF16),
@@ -363,9 +497,10 @@
             vmem((4, 2, 128, 256), BF16),
             vmem((4, 128, 256), BF16),
             vmem((4, 128, 256), BF16),
-            dma((7,)),
+            dma((8,)),
             dma((7,)), dma((7,)),
-            dma((2, 35)), dma((2, 35)),
+            dma((2, 35)), dma((2, 35)), dma((2, 4)),
+            dma((11,)), dma((11,)), dma((4,)),
             dma((4, 7)), dma((4, 7)),
         ],
         compiler_params=pltpu.CompilerParams(

time: 161 us -> 132 us (0.82)
  the two profiles are of different devices: /device:TPU:33 before, /device:TPU:1 now
where the time goes in v3:
time: 132 us
  Pallas kernels  128 us (97%)
  local copies, waits for them, and re-layouts  3.14 us (2%)
    pallas_call x1, Pallas kernels, on_device(): pl.pallas_call(kernel, out_shape=(jax.ShapeDtypeStruct((128, 1024), BF16)...  128 us
    unnamed x2, local copies, waits for them, and re-layouts  3.14 us

profile of v3, /device:TPU:1, one launch (start us, length us, event | category | flops | bytes accessed | tf_op | source)
XLA Modules:
  0.0 131.7 jit_solution(18319947927887503403)
XLA Ops:
  0.6 127.9 %layer.1 = (bf16[128,1024]{1,0:T(8,128)(2,1)}, bf16[2,2,64,128]{3,2,1,0:T(8,128)(2,1)}) custom-call(s32[32]{0:T(128)} %plan.1, s32[64]{0:T(128)} %lengths.1, bf16[128,1024]{1,0:T(8,128)(2,1)} %bitcast.7, bf16[2,64,128,128]{3,2,1,0:T(8,128)(2,1)} %bitcast.6, bf16[256,512]{1,0:T(8,128)(2,1)} %wq.1, bf16[2,256,128]{2,1,0:T(8,128)(2,1)} %wkv.1, bf16[512,256]{1,0:T(8,128)(2,1)} %wo.1), custom_call_target="tpu_custom_call" | custom-call | tf_op jit(solution)/shard_map/layer/pallas_call | solution.py:468
  128.5 1.7 %copy.12 = bf16[2,64,1024]{2,1,0:T(8,128)(2,1)} copy(bf16[2,64,1024]{2,1,0:T(8,128)(2,1)} %bitcast.8) | data formatting | bytes 524288
  130.2 1.5 %copy.13 = bf16[2,2,64,1,128]{4,2,3,1,0:T(8,128)(2,1)} copy(bf16[2,2,64,1,128]{4,2,3,1,0:T(8,128)(2,1)} %bitcast.9) | data formatting | bytes 131072

commit v4 on v3

--- a/solution.py
+++ b/solution.py
@@ -272,6 +272,8 @@
     z_out(1, 1)
     e1(1, 1)
     e3(0, 2)
+    z_out(1, 2)
+    e1(1, 2)
 
     for first, zh_ in ((1, zh), (4, 1 - zh)):
         for i, y_ in enumerate((yl, yr, yo)):
@@ -305,8 +307,6 @@
 
     project(0)
     project(1)
-    z_out(1, 2)
-    e1(1, 2)
     project(2)
     c_in(1)
     c_in(2)
@@ -362,24 +362,26 @@
     attend(0)
     attend(1)
     c_in(3)
+    e2(1, 2)
     attend(2)
     e3(1, 1)
     c_out(2)
     c_sibling(2)
     attend(3)
-    e2(1, 2)
+
     for s in range(2):
         for g in range(4):
             heads[64 * s : 64 * (s + 1), 128 * g : 128 * (g + 1)] = h8[:, 4 * s + g, :].astype(BF16)
     some_inverse(0)
+    e3(1, 2)
     some_inverse(1)
-    e3(1, 2)
+    e2(1, 3)
     some_inverse(2)
     some_inverse(3)
-    e2(1, 3)
     c_out(3)
     c_sibling(3)
     e3(1, 3)
+
     for k in range(4):
         e4(1, k)
     c4()
@@ -458,6 +460,11 @@
             for t in range(2):
                 z_copy(t, k).wait_send()
             c_copy(k).wait_send()
+
+
+def finish(sums, fresh, out, new_kv):
+    out[...] = sums[...]
+    new_kv[...] = fresh[...]
 
 
 def on_device(states, cache, lengths, plan, wq_new, wkv_new, wo_new):
@@ -511,6 +518,17 @@
         plan, lengths, states.reshape(128, 1024), cache.reshape(2, 64, 128, 128),
         wq_new, wkv_new, wo_new,
     )
+    whole = pl.BlockSpec(memory_space=pltpu.VMEM)
+    attended, new_kv = pl.pallas_call(
+        finish,
+        out_shape=(
+            jax.ShapeDtypeStruct((128, 1024), BF16),
+            jax.ShapeDtypeStruct((2, 2, 64, 128), BF16),
+        ),
+        in_specs=[whole, whole],
+        out_specs=[whole, whole],
+        name="finish",
+    )(attended, new_kv)
     return attended.reshape(2, 64, 1024), new_kv.reshape(2, 2, 64, 1, 128)
 
 

time: 132 us -> 126 us (0.955)
  Pallas kernels: 128 us -> 124 us
  local copies, waits for them, and re-layouts: 3.14 us -> 0 us
    pallas_call x1, Pallas kernels: 128 us -> 123 us  [on_device(): pl.pallas_call(kernel, out_shape=(jax.ShapeDtypeStruct((128, 1024), BF16)...]
    unnamed x2 -> x0, local copies, waits for them, and re-layouts: 3.14 us -> none
    pallas_call x0 -> x1, Pallas kernels: none -> 1.69 us  [on_device(): pl.pallas_call(finish, out_shape=(jax.ShapeDtypeStruct((128, 1024), BF16)...]
where the time goes in v4:
time: 126 us; the launch traced here: 125 us
  Pallas kernels  124 us (98%)
    pallas_call x1, Pallas kernels, on_device(): pl.pallas_call(kernel, out_shape=(jax.ShapeDtypeStruct((128, 1024), BF16)...  123 us

profile of v4, /device:TPU:1, one launch (start us, length us, event | category | flops | bytes accessed | tf_op | source)
XLA Modules:
  0.0 125.0 jit_solution(6298989966110426796)
XLA Ops:
  0.6 122.7 %layer.1 = (bf16[128,1024]{1,0:T(8,128)(2,1)}, bf16[2,2,64,128]{3,2,1,0:T(8,128)(2,1)}) custom-call(s32[32]{0:T(128)} %plan.1, s32[64]{0:T(128)} %lengths.1, bf16[128,1024]{1,0:T(8,128)(2,1)} %bitcast.7, bf16[2,64,128,128]{3,2,1,0:T(8,128)(2,1)} %bitcast.6, bf16[256,512]{1,0:T(8,128)(2,1)} %wq.1, bf16[2,256,128]{2,1,0:T(8,128)(2,1)} %wkv.1, bf16[512,256]{1,0:T(8,128)(2,1)} %wo.1), custom_call_target="tpu_custom_call" | custom-call | tf_op jit(solution)/shard_map/layer/pallas_call | solution.py:475
  123.3 1.7 %finish.1 = (bf16[128,1024]{1,0:T(8,128)(2,1)}, bf16[2,2,64,128]{3,2,1,0:T(8,128)(2,1)}) custom-call(bf16[128,1024]{1,0:T(8,128)(2,1)} %get-tuple-element.6.sums, bf16[2,2,64,128]{3,2,1,0:T(8,128)(2,1)} %get-tuple-element.7.fresh), custom_call_target="tpu_custom_call" | custom-call | tf_op jit(solution)/shard_map/finish/pallas_call | solution.py:522

commit v5 on v4

--- a/solution.py
+++ b/solution.py
@@ -19,7 +19,7 @@
     out, new_kv,
     own_q, own_kv,
     wa0, wa1, wa2, wa3, wb, wc, st, xn, xp, acc, keys, values, lens, q8, h8, heads, kvn, inverse,
-    part, from_left, from_right, transit, far_out, far_in,
+    part, from_left, from_right, transit, far_out, far_in, mine_sum,
     local_sem, st_send, st_recv, w_send, w_recv, z_send, c_send, c_recv, cz_send, r_send, r_recv,
 ):
     grp = lax.axis_index("grp")
@@ -434,6 +434,7 @@
         arrived(from_right.at[j, 1], r_recv.at[j, 5])
         far_out[j] = summed(j, 1 - zh).astype(BF16)
         r_send_to(j, 6, far_out.at[j], far_in.at[j], device(zh_=1 - zh))
+        mine_sum[j] = summed(j, zh)
 
     r1(0)
     r1(1)
@@ -447,11 +448,7 @@
     r2(3)
     r3(2)
     r3(3)
-    for j in range(4):
-        arrived(far_in.at[j], r_recv.at[j, 6])
-        out[:, 256 * j : 256 * (j + 1)] = (summed(j, zh) + far_in[j].astype(F32)).astype(BF16)
-
-    for copy in sent:
+    for copy in sent[:-4]:
         copy.wait_send()
 
     @pl.when(inner)
@@ -460,6 +457,13 @@
             for t in range(2):
                 z_copy(t, k).wait_send()
             c_copy(k).wait_send()
+
+    for j in range(4):
+        arrived(far_in.at[j], r_recv.at[j, 6])
+        out[:, 256 * j : 256 * (j + 1)] = (mine_sum[j] + far_in[j].astype(F32)).astype(BF16)
+
+    for copy in sent[-4:]:
+        copy.wait_send()
 
 
 def finish(sums, fresh, out, new_kv):
@@ -504,6 +508,7 @@
             vmem((4, 2, 128, 256), BF16),
             vmem((4, 128, 256), BF16),
             vmem((4, 128, 256), BF16),
+            vmem((4, 128, 256), F32),
             dma((8,)),
             dma((7,)), dma((7,)),
             dma((2, 35)), dma((2, 35)), dma((2, 4)),

time: 126 us -> 126 us (level)
  no operation moved by 1% of the time
where the time goes in v5:
time: 126 us; the launch traced here: 125 us
  Pallas kernels  124 us (98%)
    pallas_call x1, Pallas kernels, on_device(): pl.pallas_call(kernel, out_shape=(jax.ShapeDtypeStruct((128, 1024), BF16)...  122 us

profile of v5, /device:TPU:1, one launch (start us, length us, event | category | flops | bytes accessed | tf_op | source)
XLA Modules:
  0.0 124.7 jit_solution(17509882047180940971)
XLA Ops:
  0.6 122.4 %layer.1 = (bf16[128,1024]{1,0:T(8,128)(2,1)}, bf16[2,2,64,128]{3,2,1,0:T(8,128)(2,1)}) custom-call(s32[32]{0:T(128)} %plan.1, s32[64]{0:T(128)} %lengths.1, bf16[128,1024]{1,0:T(8,128)(2,1)} %bitcast.7, bf16[2,64,128,128]{3,2,1,0:T(8,128)(2,1)} %bitcast.6, bf16[256,512]{1,0:T(8,128)(2,1)} %wq.1, bf16[2,256,128]{2,1,0:T(8,128)(2,1)} %wkv.1, bf16[512,256]{1,0:T(8,128)(2,1)} %wo.1), custom_call_target="tpu_custom_call" | custom-call | tf_op jit(solution)/shard_map/layer/pallas_call | solution.py:479
  123.0 1.7 %finish.1 = (bf16[128,1024]{1,0:T(8,128)(2,1)}, bf16[2,2,64,128]{3,2,1,0:T(8,128)(2,1)}) custom-call(bf16[128,1024]{1,0:T(8,128)(2,1)} %get-tuple-element.6.sums, bf16[2,2,64,128]{3,2,1,0:T(8,128)(2,1)} %get-tuple-element.7.fresh), custom_call_target="tpu_custom_call" | custom-call | tf_op jit(solution)/shard_map/finish/pallas_call | solution.py:527

commit v6 on v5

--- a/solution.py
+++ b/solution.py
@@ -19,7 +19,7 @@
     out, new_kv,
     own_q, own_kv,
     wa0, wa1, wa2, wa3, wb, wc, st, xn, xp, acc, keys, values, lens, q8, h8, heads, kvn, inverse,
-    part, from_left, from_right, transit, far_out, far_in, mine_sum,
+    part, from_left, from_right, transit, far_out, far_in,
     local_sem, st_send, st_recv, w_send, w_recv, z_send, c_send, c_recv, cz_send, r_send, r_recv,
 ):
     grp = lax.axis_index("grp")
@@ -252,6 +252,7 @@
     z_in(0, 2)
     z_out(0, 1)
     e1(0, 1)
+    some_inverse(0)
     arrived(st.at[tp_far], st_recv.at[0])
     spread_states(4, tp_far)
     e3(0, 0)
@@ -259,11 +260,13 @@
     z_in(0, 3)
     z_out(0, 2)
     e1(0, 2)
+    some_inverse(1)
     e2(0, 1)
     e3(0, 1)
     z_out(0, 3)
     z_start(1)
     e1(0, 3)
+    some_inverse(2)
     z_in(1, 1)
     z_in(1, 2)
     e2(0, 2)
@@ -271,6 +274,7 @@
     c3()
     z_out(1, 1)
     e1(1, 1)
+    some_inverse(3)
     e3(0, 2)
     z_out(1, 2)
     e1(1, 2)
@@ -372,12 +376,8 @@
     for s in range(2):
         for g in range(4):
             heads[64 * s : 64 * (s + 1), 128 * g : 128 * (g + 1)] = h8[:, 4 * s + g, :].astype(BF16)
-    some_inverse(0)
     e3(1, 2)
-    some_inverse(1)
     e2(1, 3)
-    some_inverse(2)
-    some_inverse(3)
     c_out(3)
     c_sibling(3)
     e3(1, 3)
@@ -434,7 +434,6 @@
         arrived(from_right.at[j, 1], r_recv.at[j, 5])
         far_out[j] = summed(j, 1 - zh).astype(BF16)
         r_send_to(j, 6, far_out.at[j], far_in.at[j], device(zh_=1 - zh))
-        mine_sum[j] = summed(j, zh)
 
     r1(0)
     r1(1)
@@ -460,7 +459,7 @@
 
     for j in range(4):
         arrived(far_in.at[j], r_recv.at[j, 6])
-        out[:, 256 * j : 256 * (j + 1)] = (mine_sum[j] + far_in[j].astype(F32)).astype(BF16)
+        out[:, 256 * j : 256 * (j + 1)] = (summed(j, zh) + far_in[j].astype(F32)).astype(BF16)
 
     for copy in sent[-4:]:
         copy.wait_send()
@@ -508,7 +507,6 @@
             vmem((4, 2, 128, 256), BF16),
             vmem((4, 128, 256), BF16),
             vmem((4, 128, 256), BF16),
-            vmem((4, 128, 256), F32),
             dma((8,)),
             dma((7,)), dma((7,)),
             dma((2, 35)), dma((2, 35)), dma((2, 4)),

time: 126 us -> 126 us (level)
  no operation moved by 1% of the time
where the time goes in v6:
time: 126 us; the launch traced here: 125 us
  Pallas kernels  124 us (98%)
    pallas_call x1, Pallas kernels, on_device(): pl.pallas_call(kernel, out_shape=(jax.ShapeDtypeStruct((128, 1024), BF16)...  123 us

profile of v6, /device:TPU:1, one launch (start us, length us, event | category | flops | bytes accessed | tf_op | source)
XLA Modules:
  0.0 125.1 jit_solution(3760559486689753306)
XLA Ops:
  0.6 122.8 %layer.1 = (bf16[128,1024]{1,0:T(8,128)(2,1)}, bf16[2,2,64,128]{3,2,1,0:T(8,128)(2,1)}) custom-call(s32[32]{0:T(128)} %plan.1, s32[64]{0:T(128)} %lengths.1, bf16[128,1024]{1,0:T(8,128)(2,1)} %bitcast.7, bf16[2,64,128,128]{3,2,1,0:T(8,128)(2,1)} %bitcast.6, bf16[256,512]{1,0:T(8,128)(2,1)} %wq.1, bf16[2,256,128]{2,1,0:T(8,128)(2,1)} %wkv.1, bf16[512,256]{1,0:T(8,128)(2,1)} %wo.1), custom_call_target="tpu_custom_call" | custom-call | tf_op jit(solution)/shard_map/layer/pallas_call | solution.py:478
  123.4 1.7 %finish.1 = (bf16[128,1024]{1,0:T(8,128)(2,1)}, bf16[2,2,64,128]{3,2,1,0:T(8,128)(2,1)}) custom-call(bf16[128,1024]{1,0:T(8,128)(2,1)} %get-tuple-element.6.sums, bf16[2,2,64,128]{3,2,1,0:T(8,128)(2,1)} %get-tuple-element.7.fresh), custom_call_target="tpu_custom_call" | custom-call | tf_op jit(solution)/shard_map/finish/pallas_call | solution.py:525
